TPU v7x, 32 devices: a whole 2x2x4 slice. The times are simulated.
32 devices in a mesh: docs: 16 (over z, y, x), cols: 2 (over core).
Axes of the slice: x: 2, y: 2, z: 4, core: 2. Of those that a mesh axis runs over, the one named last changes fastest.
Arguments:
- blocks: bfloat16 [256, 64, 128, 128], P('docs', 'cols'), may hold values from -3 to 3
- slot_entry: int32 [256, 64], P('docs', 'cols'), may hold values from 0 to 63, as said below
- ghost_table: int32 [16, 2, 16, 4], P('docs', 'cols'), may hold values from 0 to 63, as said below
- live_counts: int32 [256, 2], P('docs', 'cols'), may hold values from 1 to 32, as said below
- test_matrix: bfloat16 [262144, 256], P(('docs', 'cols')), may hold values from -6 to 6
Outputs:
- basis_rows: bfloat16 [32768, 256], P('docs')
- projected: bfloat16 [256, 262144], P(None, ('docs', 'cols'))
Inputs may be any that keep to these rules, and one draw needn't show every extreme that they name: `slot_entry`: the 32 entries of one block row in one half are distinct. `ghost_table`: for each d, c and o the 4 entries are distinct. `live_counts`: every index of docs has, in each half, a block row with all 32 slots live.
All inputs are finite; a program needn't handle non-finite values.
Results may differ from a plain program's by a relative error of at most 0.0055.
Values may be sent and summed in bfloat16 or wider, within the bound.
A program may use at most 256 MiB of HBM per device.

v0:
```python
import jax
import jax.numpy as jnp
from jax import lax
from jax.sharding import PartitionSpec as P


def gram_of(rows_block):
    return lax.dot_general(
        rows_block, rows_block, (((0,), (0,)), ((), ())), precision=lax.Precision.HIGHEST
    )


def orthonormal(rows_block, gram):
    lower = jnp.linalg.cholesky(gram)
    solved = lax.linalg.triangular_solve(lower, rows_block.T, left_side=True, lower=True)
    return solved.T.astype(jnp.bfloat16)


def on_device(blocks, slot_entry, ghost_table, live_counts, test_matrix):
    block_rows, slot_count, block_edge, _ = blocks.shape
    sketch_width = test_matrix.shape[1]
    owners = lax.axis_size("docs")
    table = ghost_table.reshape(owners, ghost_table.shape[-1])
    per_owner = table.shape[1]
    entries = owners * per_owner
    active = (jnp.arange(slot_count, dtype=jnp.int32)[None, :] < live_counts).astype(blocks.dtype)
    requests = lax.all_to_all(table, "docs", split_axis=0, concat_axis=0, tiled=True)
    local_pieces = test_matrix.reshape(-1, block_edge, sketch_width)
    fetched = lax.all_to_all(
        local_pieces[requests], "docs", split_axis=0, concat_axis=0, tiled=True
    )
    fetched = fetched.reshape(entries, block_edge, sketch_width)

    def sketch_row(carry, inputs):
        stored, chosen, weights = inputs
        masked = stored * weights[:, None, None]
        return (
            carry,
            jnp.einsum("sij,sjk->ik", masked, fetched[chosen], preferred_element_type=jnp.float32),
        )

    _, partial_rows = lax.scan(sketch_row, jnp.int32(0), (blocks, slot_entry, active))
    partial_value = partial_rows.reshape(block_rows * block_edge, sketch_width)
    sketch = lax.psum(partial_value, "cols")
    gram = lax.psum(gram_of(sketch), "docs")
    basis_rows = orthonormal(sketch, gram)
    basis_blocks = basis_rows.reshape(block_rows, block_edge, sketch_width)

    def project_row(total, inputs):
        stored, chosen, weights, rows_here = inputs
        masked = stored * weights[:, None, None]
        terms = jnp.einsum("ib,sij->sbj", rows_here, masked, preferred_element_type=jnp.float32)
        return (total.at[chosen].add(terms), None)

    start = jnp.zeros((entries, sketch_width, block_edge), jnp.float32)
    total, _ = lax.scan(project_row, start, (blocks, slot_entry, active, basis_blocks))
    outgoing = total.astype(jnp.bfloat16).reshape(owners, per_owner, sketch_width, block_edge)
    incoming = lax.all_to_all(outgoing, "docs", split_axis=0, concat_axis=0, tiled=True)
    owned = jnp.zeros((test_matrix.shape[0] // block_edge, sketch_width, block_edge), jnp.float32)
    owned = owned.at[requests.reshape(-1)].add(
        incoming.reshape(-1, sketch_width, block_edge).astype(jnp.float32)
    )
    projected = owned.transpose(1, 0, 2).reshape(sketch_width, -1).astype(jnp.bfloat16)
    return (basis_rows, projected)


def solution(mesh):
    in_specs = (
        P("docs", "cols", None, None),
        P("docs", "cols"),
        P("docs", "cols", None, None),
        P("docs", "cols"),
        P(("docs", "cols"), None),
    )
    out_specs = (P("docs", None), P(None, ("docs", "cols")))
    return jax.shard_map(
        on_device, mesh=mesh, in_specs=in_specs, out_specs=out_specs, check_vma=False
    )
```

profile of v0, /device:TPU:14, one launch (start us, length us, event | category | flops | bytes accessed | tf_op | source)
XLA Modules:
  0.0 911.2 jit_solution(16879464373417153344)
XLA Ops:
  7.9 11.1 %all_to_all.22 = s32[16,1,4]{2,1,0:T(1,128)S(1)} all-to-all(s32[16,1,4]{2,1,0:T(1,128)S(1)} %copy.26), channel_id=1, replica_groups=mesh['docs'=16,'cols'=2] {'docs'}, dimensions={0} | all-to-all | bytes 512 | tf_op jit(solution)/shard_map/all_to_all | solution.py:27
  32.1 92.0 %all-to-all-done.1 = bf16[16,4,128,256]{3,2,1,0:T(8,128)(2,1)} async-done(((bf16[16,4,128,256]{3,2,1,0:T(8,128)(2,1)}), bf16[16,4,128,256]{3,2,1,0:T(8,128)(2,1)}, u32[]{:S(2)}, u32[]{:S(2)}) %all-to-all-start.1) | async-done | bytes 4194336 | tf_op jit(solution)/shard_map/all_to_all | solution.py:29
  124.1 95.4 %while.21 = (s32[]{:T(128)}, f32[16,128,256]{2,1,0:T(8,128)}, bf16[16,32,128,128]{3,2,1,0:T(8,128)(2,1)}, bf16[16,32]{1,0:T(8,128)(2,1)S(1)}, s32[16,32]{1,0:T(8,128)}, /*index=5*/bf16[64,128,256]{2,1,0:T(8,128)(2,1)}, s32[]{:T(128)}) while((s32[]{:T(128)}, f32[16,128,256]{2,1,0:T(8,128)}, bf16[16,32,128,128]{3,2,1,0:T(8,128)(2,1)}, ...), condition=%wide.region_1.2_spmd, body=%wide.region_0.1_spmd.sunk | while | flops 268960864 | bytes 7477021 | solution.py:42
  222.4 20.7 %all-reduce.4.cloned.1.call-done = f32[2048,256]{0,1:T(8,128)} async-done(((f32[2048,256]{0,1:T(8,128)}), f32[2048,256]{0,1:T(8,128)}) %all-reduce.4.cloned.1.call-update) | async-done | bytes 2097168 | tf_op jit(solution)/shard_map/psum | solution.py:44
  248.1 108.6 %all-reduce.6.cloned.1.call-done = f32[256,256]{0,1:T(8,128)} async-done(((f32[256,256]{0,1:T(8,128)}), f32[256,256]{0,1:T(8,128)}) %all-reduce.6.cloned.1.call-update) | async-done | bytes 262160 | tf_op jit(solution)/shard_map/psum | solution.py:45
  358.7 11.7 %cholesky.50 = f32[128,128]{1,0:T(8,128)S(1)} custom-call(f32[128,128]{1,0:T(8,128)S(1)} %cholesky.118), custom_call_target="Cholesky" | custom-call | tf_op jit(solution)/shard_map/jit(cholesky)/cholesky | solution.py:14
  380.8 11.8 %cholesky.105 = f32[128,128]{1,0:T(8,128)S(1)} custom-call(f32[128,128]{1,0:T(8,128)S(1)} %convolution_subtract_fusion.1), custom_call_target="Cholesky" | custom-call | tf_op jit(solution)/shard_map/jit(cholesky)/cholesky | solution.py:14
  398.6 19.7 %custom-call.15 = f32[2,128,128]{1,2,0:T(8,128)S(1)} custom-call(f32[2,128,128]{2,1,0:T(8,128)S(1)} %get-tuple-element.75), custom_call_target="InvertDiagBlocksLowerTriangular" | custom-call | tf_op jit(solution)/shard_map/triangular_solve | solution.py:15
  426.3 338.4 %while.22 = (s32[]{:T(128)}, f32[64,256,128]{2,1,0:T(8,128)}, s32[16,32]{1,0:T(8,128)}, bf16[16,32,128,128]{3,2,1,0:T(8,128)(2,1)}, bf16[16,32]{1,0:T(8,128)(2,1...) while((s32[]{:T(128)}, f32[64,256,128]{2,1,0:T(8,128)}, s32[16,32]{1,0:T(8,128)}, ...), condition=%wide.region_10.11_spmd, body=%wide.region_8.10_spmd.sunk | while | flops 270008416 | bytes 30475364 | solution.py:56
  437.3 10.1 %scatter_fusion = f32[64,256,128]{2,1,0:T(8,128)} fusion(f32[64,256,128]{2,1,0:T(8,128)} %get-tuple-element.291, s32[32]{0:T(128)S(1)} %fusion.50, f32[32,256,128]{2,1,0:T(8,128)} %copy.45), kind=kCustom, calls=%fused_computation.2.clone.1 | custom fusion | flops 1048576 | bytes 12583040 | tf_op jit(solution)/shard_map/while/body/eval_jaxpr/scatter-add | solution.py:53
  479.5 10.2 %scatter_fusion = f32[64,256,128]{2,1,0:T(8,128)} fusion(f32[64,256,128]{2,1,0:T(8,128)} %get-tuple-element.291, s32[32]{0:T(128)S(1)} %fusion.50, f32[32,256,128]{2,1,0:T(8,128)} %copy.45), kind=kCustom, calls=%fused_computation.2.clone.1 | custom fusion | flops 1048576 | bytes 12583040 | tf_op jit(solution)/shard_map/while/body/eval_jaxpr/scatter-add | solution.py:53
  500.7 10.2 %scatter_fusion = f32[64,256,128]{2,1,0:T(8,128)} fusion(f32[64,256,128]{2,1,0:T(8,128)} %get-tuple-element.291, s32[32]{0:T(128)S(1)} %fusion.50, f32[32,256,128]{2,1,0:T(8,128)} %copy.45), kind=kCustom, calls=%fused_computation.2.clone.1 | custom fusion | flops 1048576 | bytes 12583040 | tf_op jit(solution)/shard_map/while/body/eval_jaxpr/scatter-add | solution.py:53
  521.9 10.2 %scatter_fusion = f32[64,256,128]{2,1,0:T(8,128)} fusion(f32[64,256,128]{2,1,0:T(8,128)} %get-tuple-element.291, s32[32]{0:T(128)S(1)} %fusion.50, f32[32,256,128]{2,1,0:T(8,128)} %copy.45), kind=kCustom, calls=%fused_computation.2.clone.1 | custom fusion | flops 1048576 | bytes 12583040 | tf_op jit(solution)/shard_map/while/body/eval_jaxpr/scatter-add | solution.py:53
  564.2 10.1 %scatter_fusion = f32[64,256,128]{2,1,0:T(8,128)} fusion(f32[64,256,128]{2,1,0:T(8,128)} %get-tuple-element.291, s32[32]{0:T(128)S(1)} %fusion.50, f32[32,256,128]{2,1,0:T(8,128)} %copy.45), kind=kCustom, calls=%fused_computation.2.clone.1 | custom fusion | flops 1048576 | bytes 12583040 | tf_op jit(solution)/shard_map/while/body/eval_jaxpr/scatter-add | solution.py:53
  585.3 10.1 %scatter_fusion = f32[64,256,128]{2,1,0:T(8,128)} fusion(f32[64,256,128]{2,1,0:T(8,128)} %get-tuple-element.291, s32[32]{0:T(128)S(1)} %fusion.50, f32[32,256,128]{2,1,0:T(8,128)} %copy.45), kind=kCustom, calls=%fused_computation.2.clone.1 | custom fusion | flops 1048576 | bytes 12583040 | tf_op jit(solution)/shard_map/while/body/eval_jaxpr/scatter-add | solution.py:53
  606.5 10.1 %scatter_fusion = f32[64,256,128]{2,1,0:T(8,128)} fusion(f32[64,256,128]{2,1,0:T(8,128)} %get-tuple-element.291, s32[32]{0:T(128)S(1)} %fusion.50, f32[32,256,128]{2,1,0:T(8,128)} %copy.45), kind=kCustom, calls=%fused_computation.2.clone.1 | custom fusion | flops 1048576 | bytes 12583040 | tf_op jit(solution)/shard_map/while/body/eval_jaxpr/scatter-add | solution.py:53
  627.6 10.2 %scatter_fusion = f32[64,256,128]{2,1,0:T(8,128)} fusion(f32[64,256,128]{2,1,0:T(8,128)} %get-tuple-element.291, s32[32]{0:T(128)S(1)} %fusion.50, f32[32,256,128]{2,1,0:T(8,128)} %copy.45), kind=kCustom, calls=%fused_computation.2.clone.1 | custom fusion | flops 1048576 | bytes 12583040 | tf_op jit(solution)/shard_map/while/body/eval_jaxpr/scatter-add | solution.py:53
  669.9 10.2 %scatter_fusion = f32[64,256,128]{2,1,0:T(8,128)} fusion(f32[64,256,128]{2,1,0:T(8,128)} %get-tuple-element.291, s32[32]{0:T(128)S(1)} %fusion.50, f32[32,256,128]{2,1,0:T(8,128)} %copy.45), kind=kCustom, calls=%fused_computation.2.clone.1 | custom fusion | flops 1048576 | bytes 12583040 | tf_op jit(solution)/shard_map/while/body/eval_jaxpr/scatter-add | solution.py:53
  691.0 10.1 %scatter_fusion = f32[64,256,128]{2,1,0:T(8,128)} fusion(f32[64,256,128]{2,1,0:T(8,128)} %get-tuple-element.291, s32[32]{0:T(128)S(1)} %fusion.50, f32[32,256,128]{2,1,0:T(8,128)} %copy.45), kind=kCustom, calls=%fused_computation.2.clone.1 | custom fusion | flops 1048576 | bytes 12583040 | tf_op jit(solution)/shard_map/while/body/eval_jaxpr/scatter-add | solution.py:53
  712.2 10.2 %scatter_fusion = f32[64,256,128]{2,1,0:T(8,128)} fusion(f32[64,256,128]{2,1,0:T(8,128)} %get-tuple-element.291, s32[32]{0:T(128)S(1)} %fusion.50, f32[32,256,128]{2,1,0:T(8,128)} %copy.45), kind=kCustom, calls=%fused_computation.2.clone.1 | custom fusion | flops 1048576 | bytes 12583040 | tf_op jit(solution)/shard_map/while/body/eval_jaxpr/scatter-add | solution.py:53
  733.4 10.1 %scatter_fusion = f32[64,256,128]{2,1,0:T(8,128)} fusion(f32[64,256,128]{2,1,0:T(8,128)} %get-tuple-element.291, s32[32]{0:T(128)S(1)} %fusion.50, f32[32,256,128]{2,1,0:T(8,128)} %copy.45), kind=kCustom, calls=%fused_computation.2.clone.1 | custom fusion | flops 1048576 | bytes 12583040 | tf_op jit(solution)/shard_map/while/body/eval_jaxpr/scatter-add | solution.py:53
  754.5 10.2 %scatter_fusion = f32[64,256,128]{2,1,0:T(8,128)} fusion(f32[64,256,128]{2,1,0:T(8,128)} %get-tuple-element.291, s32[32]{0:T(128)S(1)} %fusion.50, f32[32,256,128]{2,1,0:T(8,128)} %copy.45), kind=kCustom, calls=%fused_computation.2.clone.1 | custom fusion | flops 1048576 | bytes 12583040 | tf_op jit(solution)/shard_map/while/body/eval_jaxpr/scatter-add | solution.py:53
  778.8 89.3 %all-to-all-done.2 = bf16[16,4,256,128]{3,2,1,0:T(8,128)(2,1)} async-done(((bf16[16,4,256,128]{3,2,1,0:T(8,128)(2,1)}), bf16[16,4,256,128]{3,2,1,0:T(8,128)(2,1)}, u32[]{:S(2)}, u32[]{:S(2)}) %all-to-all-start.2) | async-done | bytes 4194336 | tf_op jit(solution)/shard_map/all_to_all | solution.py:58
  878.9 19.4 %scatter_fusion.1 = f32[64,256,128]{2,1,0:T(8,128)} fusion(f32[64,256,128]{2,1,0:T(8,128)} %broadcast.166, s32[64]{0:T(128)S(1)} %fusion.24, f32[64,256,128]{2,1,0:T(8,128)} %bitcast_convert_fusion), kind=kCustom, calls=%fused_computation.3 | custom fusion | flops 2097152 | bytes 25166080 | tf_op jit(solution)/shard_map/scatter-add | solution.py:60
  (237 shorter events, 382.7 us)
Async XLA Ops:
  24.3 7.7 copy-start.2
  24.3 99.8 %all-to-all-start.1 = ((bf16[16,4,128,256]{3,2,1,0:T(8,128)(2,1)}), bf16[16,4,128,256]{3,2,1,0:T(8,128)(2,1)}, u32[]{:S(2)}, u32[]{:S(2)}) async-start(bf16[16,4,128,256]{3,2,1,0:T(8,128)(2,1)} %bitcast.126), calls=%async_computation.1 | async-start | bytes 8388608 | tf_op jit(solution)/shard_map/all_to_all | solution.py:29
  31.9 211.1 %all-reduce.4.cloned.1.call-start = ((), (), s32[]{:S(2)}) async-start(), calls=%async_computation.3 | async-start | bytes 4194304 | tf_op jit(solution)/shard_map/psum | solution.py:44
  222.4 134.2 %all-reduce.6.cloned.1.call-start = ((), (), s32[]{:S(2)}) async-start(), calls=%async_computation.4 | async-start | bytes 524288 | tf_op jit(solution)/shard_map/psum | solution.py:45
  243.1 175.2 %copy-start = (f32[2048,256]{0,1:T(8,128)S(1)}, f32[2048,256]{0,1:T(8,128)}, u32[]{:S(2)}) copy-start(f32[2048,256]{0,1:T(8,128)} %all-reduce.4.cloned.1.call-done) | copy-start | bytes 6291460
  764.7 6.5 copy-start.1
  771.2 96.9 %all-to-all-start.2 = ((bf16[16,4,256,128]{3,2,1,0:T(8,128)(2,1)}), bf16[16,4,256,128]{3,2,1,0:T(8,128)(2,1)}, u32[]{:S(2)}, u32[]{:S(2)}) async-start(bf16[16,4,256,128]{3,2,1,0:T(8,128)(2,1)} %bitcast.125), calls=%async_computation.2 | async-start | bytes 8388608 | tf_op jit(solution)/shard_map/all_to_all | solution.py:58
Sparse Core Ops, SparseCore 0:
  222.5 20.5 all-reduce.3
  249.7 106.8 all-reduce.5
where the time goes:
time: 917 us; the launch traced here: 911 us
  waiting for transfers between devices  311 us (34%)
  other arithmetic  279 us (30%)
  local copies, waits for them, and re-layouts  190 us (21%)
  matrix products  90.7 us (10%)
  between operations  15.5 us (2%)
  starting transfers between devices  13.9 us (2%)
  blocking collectives  11.1 us (1%)
    scatter-add x16, other arithmetic, project_row(): return (total.at[chosen].add(terms), None)  162 us
    psum x1, waiting for transfers between devices, on_device(): gram = lax.psum(gram_of(sketch), 'docs')  109 us
    all_to_all x1, waiting for transfers between devices, on_device(): lax.all_to_all(local_pieces[requests], 'docs', split_axis=0, concat_axis=...  92 us
    all_to_all x1, waiting for transfers between devices, on_device(): lax.all_to_all(outgoing, 'docs', split_axis=0, concat_axis=0, tiled=True)  89.3 us
    transpose x16, local copies, waits for them, and re-layouts, project_row(): jnp.einsum('ib,sij->sbj', rows_here, masked, preferred_element_type=jnp.f...  89 us
    gather x16, local copies, waits for them, and re-layouts, sketch_row(): fetched[chosen]  45.9 us
    dot_general x16, matrix products, project_row(): jnp.einsum('ib,sij->sbj', rows_here, masked, preferred_element_type=jnp.f...  44.3 us
    dot_general x16, matrix products, sketch_row(): jnp.einsum('sij,sjk->ik', masked, fetched[chosen], preferred_element_type...  37.9 us
  transfers between devices with their start and end apart: 4, of which 4 were waited for; matrix products, arithmetic and copies ran while one was open for 0% of the time, Pallas kernels for 0%

commit v1 on v0

v1 whole, which is shorter than its diff:
```python
import functools

import jax
import jax.numpy as jnp
from jax import lax
from jax.experimental import pallas as pl
from jax.experimental.pallas import tpu as pltpu
from jax.sharding import PartitionSpec as P

VMEM_BYTES = 60 * 1024 * 1024
SKETCH_GROUP = 8
PROJECT_GROUP = 4


def gram_of(rows_block):
    return lax.dot_general(
        rows_block, rows_block, (((0,), (0,)), ((), ())), precision=lax.Precision.HIGHEST
    )


def live_block(blocks_ref, k, live):
    stored = blocks_ref[0, k]
    return jnp.where(k < live, stored, jnp.zeros_like(stored))


def sketch_kernel(live_ref, entry_ref, blocks_ref, fetched_ref, out_ref):
    row = pl.program_id(0)
    live = live_ref[row]
    out_ref[...] = jnp.zeros_like(out_ref)

    def body(group, carry):
        first = group * SKETCH_GROUP
        slots = [first + i for i in range(SKETCH_GROUP)]
        stored = jnp.concatenate([live_block(blocks_ref, k, live) for k in slots], axis=1)
        pieces = jnp.concatenate([fetched_ref[entry_ref[row, k]] for k in slots], axis=0)
        out_ref[...] += jnp.dot(stored, pieces, preferred_element_type=jnp.float32)
        return carry

    lax.fori_loop(0, (live + SKETCH_GROUP - 1) // SKETCH_GROUP, body, 0)


def sketch_terms(live, slot_entry, blocks, fetched):
    block_rows, slots, edge, _ = blocks.shape
    width = fetched.shape[-1]
    return pl.pallas_call(
        sketch_kernel,
        out_shape=jax.ShapeDtypeStruct((block_rows * edge, width), jnp.float32),
        grid_spec=pltpu.PrefetchScalarGridSpec(
            num_scalar_prefetch=2,
            grid=(block_rows,),
            in_specs=[
                pl.BlockSpec((1, slots, edge, edge), lambda r, *_: (r, 0, 0, 0)),
                pl.BlockSpec(memory_space=pltpu.VMEM),
            ],
            out_specs=pl.BlockSpec((edge, width), lambda r, *_: (r, 0)),
        ),
        compiler_params=pltpu.CompilerParams(vmem_limit_bytes=VMEM_BYTES),
        name="sketch_terms",
    )(live, slot_entry, blocks, fetched)


def project_kernel(live_ref, entry_ref, blocks_ref, basis_ref, out_ref, total):
    row = pl.program_id(0)
    edge = blocks_ref.shape[-1]
    live = live_ref[row]

    @pl.when(row == 0)
    def _():
        @pl.loop(0, total.shape[0])
        def _(e):
            total[e] = jnp.zeros(total.shape[1:], total.dtype)

    basis = basis_ref[...]

    def body(group, carry):
        first = group * PROJECT_GROUP
        slots = [first + i for i in range(PROJECT_GROUP)]
        stored = jnp.concatenate([live_block(blocks_ref, k, live) for k in slots], axis=1)
        terms = jnp.dot(basis, stored, preferred_element_type=jnp.float32)
        for i, k in enumerate(slots):
            total[entry_ref[row, k]] += terms[:, i * edge : (i + 1) * edge]
        return carry

    lax.fori_loop(0, (live + PROJECT_GROUP - 1) // PROJECT_GROUP, body, 0)

    @pl.when(row == pl.num_programs(0) - 1)
    def _():
        @pl.loop(0, total.shape[0])
        def _(e):
            out_ref[e] = total[e].astype(out_ref.dtype)


def project_terms(live, slot_entry, blocks, basis, entries):
    block_rows, slots, edge, _ = blocks.shape
    width = basis.shape[0]
    return pl.pallas_call(
        project_kernel,
        out_shape=jax.ShapeDtypeStruct((entries, width, edge), jnp.bfloat16),
        grid_spec=pltpu.PrefetchScalarGridSpec(
            num_scalar_prefetch=2,
            grid=(block_rows,),
            in_specs=[
                pl.BlockSpec((1, slots, edge, edge), lambda r, *_: (r, 0, 0, 0)),
                pl.BlockSpec((width, edge), lambda r, *_: (0, r)),
            ],
            out_specs=pl.BlockSpec(memory_space=pltpu.VMEM),
            scratch_shapes=[pltpu.VMEM((entries, width, edge), jnp.float32)],
        ),
        compiler_params=pltpu.CompilerParams(vmem_limit_bytes=VMEM_BYTES),
        name="project_terms",
    )(live, slot_entry, blocks, basis)


def owner_sum_kernel(goal_ref, incoming_ref, out_ref, total):
    edge = incoming_ref.shape[-1]

    @pl.loop(0, total.shape[0])
    def _(b):
        total[b] = jnp.zeros(total.shape[1:], total.dtype)

    @pl.loop(0, incoming_ref.shape[0])
    def _(i):
        total[goal_ref[i]] += incoming_ref[i].astype(jnp.float32)

    for b in range(total.shape[0]):
        out_ref[:, b * edge : (b + 1) * edge] = total[b].astype(out_ref.dtype)


def owner_sum(goal, incoming, owned_blocks):
    _, width, edge = incoming.shape
    return pl.pallas_call(
        owner_sum_kernel,
        out_shape=jax.ShapeDtypeStruct((width, owned_blocks * edge), jnp.bfloat16),
        in_specs=[
            pl.BlockSpec(memory_space=pltpu.SMEM),
            pl.BlockSpec(memory_space=pltpu.VMEM),
        ],
        out_specs=pl.BlockSpec(memory_space=pltpu.VMEM),
        scratch_shapes=[pltpu.VMEM((owned_blocks, width, edge), jnp.float32)],
        compiler_params=pltpu.CompilerParams(vmem_limit_bytes=VMEM_BYTES),
        name="owner_sum",
    )(goal, incoming)


def docs_sum(value):
    owners = lax.axis_size("docs")
    step = 1
    while step < owners:
        value = value + lax.ppermute(value, "docs", [(i, i ^ step) for i in range(owners)])
        step *= 2
    return value


def on_device(blocks, slot_entry, ghost_table, live_counts, test_matrix):
    block_rows, slot_count, block_edge, _ = blocks.shape
    sketch_width = test_matrix.shape[1]
    owners = lax.axis_size("docs")
    table = ghost_table.reshape(owners, ghost_table.shape[-1])
    per_owner = table.shape[1]
    entries = owners * per_owner
    live = live_counts.reshape(block_rows)
    requests = lax.all_to_all(table, "docs", split_axis=0, concat_axis=0, tiled=True)
    local_pieces = test_matrix.reshape(-1, block_edge, sketch_width)
    fetched = lax.all_to_all(
        local_pieces[requests], "docs", split_axis=0, concat_axis=0, tiled=True
    )
    fetched = fetched.reshape(entries, block_edge, sketch_width)

    terms = sketch_terms(live, slot_entry, blocks, fetched)
    sketch = terms + lax.ppermute(terms, "cols", [(0, 1), (1, 0)])
    gram = docs_sum(gram_of(sketch))
    lower = jnp.linalg.cholesky(gram)
    basis = lax.linalg.triangular_solve(lower, sketch.T, left_side=True, lower=True)
    basis = basis.astype(jnp.bfloat16)
    basis_rows = basis.T

    outgoing = project_terms(live, slot_entry, blocks, basis, entries)
    incoming = lax.all_to_all(
        outgoing.reshape(owners, per_owner, sketch_width, block_edge),
        "docs", split_axis=0, concat_axis=0, tiled=True,
    )
    projected = owner_sum(
        requests.reshape(-1),
        incoming.reshape(-1, sketch_width, block_edge),
        test_matrix.shape[0] // block_edge,
    )
    return (basis_rows, projected)


def solution(mesh):
    in_specs = (
        P("docs", "cols", None, None),
        P("docs", "cols"),
        P("docs", "cols", None, None),
        P("docs", "cols"),
        P(("docs", "cols"), None),
    )
    out_specs = (P("docs", None), P(None, ("docs", "cols")))
    return jax.shard_map(
        on_device, mesh=mesh, in_specs=in_specs, out_specs=out_specs, check_vma=False
    )
```

time: 917 us -> 389 us (0.42)
  other arithmetic: 279 us -> 59.1 us
  waiting for transfers between devices: 311 us -> 121 us
  local copies, waits for them, and re-layouts: 190 us -> 12.6 us
  blocking collectives: 11.1 us -> 109 us
  matrix products: 90.7 us -> 11 us
  Pallas kernels: 0 us -> 59.5 us
  between operations: 15.5 us -> 2.04 us
    scatter-add x17 -> x0, other arithmetic: 182 us -> none  [the longest x16 162 us: project_row(): return (total.at[chosen].add(terms), None)]
    psum x2 -> x0, waiting for transfers between devices: 129 us -> none  [the longest x1 109 us: on_device(): gram = lax.psum(gram_of(sketch), 'docs')]
    all_to_all x0 -> x1, blocking collectives: none -> 98.2 us  [on_device(): lax.all_to_all(local_pieces[requests], 'docs', split_axis=0, concat_axis=...]
    all_to_all x2 -> x1, waiting for transfers between devices: 181 us -> 90.3 us  [on_device(): lax.all_to_all(outgoing.reshape(owners, per_owner, sketch_width, block_ed...]
    transpose x16 -> x0, local copies, waits for them, and re-layouts: 89 us -> none  [project_row(): jnp.einsum('ib,sij->sbj', rows_here, masked, preferred_element_type=jnp.f...]
    dot_general x32 -> x0, matrix products: 82.2 us -> none  [the longest x16 44.3 us: project_row(): jnp.einsum('ib,sij->sbj', rows_here, masked, preferred_element_type=jnp.f...]
    pallas_call x0 -> x3, Pallas kernels: none -> 59.5 us  [the longest x1 31.8 us: project_terms(): pl.pallas_call(project_kernel, out_shape=jax.ShapeDtypeStruct((entries, w...]
    gather x16 -> x0, local copies, waits for them, and re-layouts: 45.9 us -> none  [sketch_row(): fetched[chosen]]
  transfers between devices with their start and end apart: 4 -> 6, of which waited for: 4 -> 6; matrix products, arithmetic and copies ran while one was open for 0% -> 2% of each run, Pallas kernels for 0% -> 0%
where the time goes in v1:
time: 389 us; the launch traced here: 387 us
  waiting for transfers between devices  121 us (31%)
  blocking collectives  109 us (28%)
  Pallas kernels  59.5 us (15%)
  other arithmetic  59.1 us (15%)
  local copies, waits for them, and re-layouts  12.6 us (3%)
  starting transfers between devices  11.8 us (3%)
  matrix products  11 us (3%)
    all_to_all x1, blocking collectives, on_device(): lax.all_to_all(local_pieces[requests], 'docs', split_axis=0, concat_axis=...  98.2 us
    all_to_all x1, waiting for transfers between devices, on_device(): lax.all_to_all(outgoing.reshape(owners, per_owner, sketch_width, block_ed...  90.3 us
    another operation x6, other arithmetic, on_device(): lower = jnp.linalg.cholesky(gram)  34.2 us
    pallas_call x1, Pallas kernels, project_terms(): pl.pallas_call(project_kernel, out_shape=jax.ShapeDtypeStruct((entries, w...  31.8 us
    ppermute x4, waiting for transfers between devices, docs_sum(): lax.ppermute(value, 'docs', [(i, i ^ step) for i in range(owners)])  26.6 us
    another operation x4, other arithmetic, on_device(): lax.linalg.triangular_solve(lower, sketch.T, left_side=True, lower=True)  20.9 us
    pallas_call x1, Pallas kernels, sketch_terms(): pl.pallas_call(sketch_kernel, out_shape=jax.ShapeDtypeStruct((block_rows...  20.9 us
    all_to_all x1, blocking collectives, on_device(): lax.all_to_all(table, 'docs', split_axis=0, concat_axis=0, tiled=True)  11.1 us
  transfers between devices with their start and end apart: 6, of which 6 were waited for; matrix products, arithmetic and copies ran while one was open for 2% of the time, Pallas kernels for 0%

profile of v1, /device:TPU:14, one launch (start us, length us, event | category | flops | bytes accessed | tf_op | source)
XLA Modules:
  0.0 386.7 jit_solution(3648709403200999688)
XLA Ops:
  1.4 11.1 %all_to_all.22 = s32[16,1,4]{2,1,0:T(1,128)S(1)} all-to-all(s32[16,1,4]{2,1,0:T(1,128)S(1)} %copy.19), channel_id=1, replica_groups=mesh['docs'=16,'cols'=2] {'docs'}, dimensions={0} | all-to-all | bytes 512 | tf_op jit(solution)/shard_map/all_to_all | solution.py:162
  12.7 5.0 %gather_fusion = bf16[64,128,256]{2,1,0:T(8,128)(2,1)} fusion(bf16[64,128,256]{2,1,0:T(8,128)(2,1)} %bitcast.50, s32[1024]{0:T(1024)S(1)} %pad_clamp_fusion), kind=kCustom, calls=%fused_computation | custom fusion | bytes 8388864 | tf_op jit(solution)/shard_map/gather | solution.py:165
  17.7 98.2 %all_to_all.23 = bf16[16,4,128,256]{3,2,1,0:T(8,128)(2,1)} all-to-all(bf16[16,4,128,256]{3,2,1,0:T(8,128)(2,1)} %bitcast.47), channel_id=1, replica_groups=mesh['docs'=16,'cols'=2] {'docs'}, dimensions={0} | all-to-all | bytes 8388608 | tf_op jit(solution)/shard_map/all_to_all | solution.py:164
  116.0 20.9 %sketch_terms.1 = f32[2048,256]{1,0:T(8,128)} custom-call(s32[16]{0:T(128)} %bitcast.51, s32[16,32]{1,0:T(8,128)} %entry_ref.3, bf16[16,32,128,128]{3,2,1,0:T(8,128)(2,1)} %blocks_ref.3, bf16[64,128,256]{2,1,0:T(8,128)(2,1)} %bitcast.49), custom_call_target="tpu_custom_call" | custom-call | tf_op jit(solution)/shard_map/sketch_terms/pallas_call | solution.py:45
  136.9 4.4 %collective-permute-done = f32[2048,256]{1,0:T(8,128)S(1)} collective-permute-done((f32[2048,256]{1,0:T(8,128)}, f32[2048,256]{1,0:T(8,128)S(1)}, u32[]{:S(2)}, u32[]{:S(2)}) %collective-permute-start) | collective-permute-done | bytes 2097184 | tf_op jit(solution)/shard_map/ppermute | solution.py:170
  141.3 6.6 %fusion.2 = f32[256,256]{0,1:T(8,128)S(1)} fusion(f32[2048,256]{1,0:T(8,128)} %sketch_terms.1, f32[2048,256]{1,0:T(8,128)S(1)} %collective-permute-done), kind=kOutput, calls=%fused_computation.9 | convolution fusion | flops 1611137024 | bytes 4456448 | tf_op jit(solution)/shard_map/dot_general | solution.py:16
  148.1 8.2 %collective-permute-done.1 = f32[256,256]{0,1:T(8,128)S(1)} collective-permute-done((f32[256,256]{0,1:T(8,128)S(1)}, f32[256,256]{0,1:T(8,128)S(1)}, u32[]{:S(2)}, u32[]{:S(2)}) %collective-permute-start.1) | collective-permute-done | bytes 262176 | tf_op jit(solution)/shard_map/ppermute | solution.py:149
  157.1 6.8 %collective-permute-done.2 = f32[256,256]{0,1:T(8,128)S(1)} collective-permute-done((f32[256,256]{0,1:T(8,128)S(1)}, f32[256,256]{0,1:T(8,128)S(1)}, u32[]{:S(2)}, u32[]{:S(2)}) %collective-permute-start.2) | collective-permute-done | bytes 262176 | tf_op jit(solution)/shard_map/ppermute | solution.py:149
  164.7 6.0 %collective-permute-done.3 = f32[256,256]{0,1:T(8,128)S(1)} collective-permute-done((f32[256,256]{0,1:T(8,128)S(1)}, f32[256,256]{0,1:T(8,128)S(1)}, u32[]{:S(2)}, u32[]{:S(2)}) %collective-permute-start.3) | collective-permute-done | bytes 262176 | tf_op jit(solution)/shard_map/ppermute | solution.py:149
  171.5 3.2 add_bitcast_fusion
  174.7 5.6 %collective-permute-done.4 = f32[256,256]{0,1:T(8,128)S(1)} collective-permute-done((f32[256,256]{0,1:T(8,128)S(1)}, f32[256,256]{0,1:T(8,128)S(1)}, u32[]{:S(2)}, u32[]{:S(2)}) %collective-permute-start.4) | collective-permute-done | bytes 262176 | tf_op jit(solution)/shard_map/ppermute | solution.py:149
  180.6 11.7 %cholesky.50 = f32[128,128]{1,0:T(8,128)S(1)} custom-call(f32[128,128]{1,0:T(8,128)S(1)} %cholesky.118), custom_call_target="Cholesky" | custom-call | tf_op jit(solution)/shard_map/jit(cholesky)/cholesky | solution.py:172
  192.3 9.8 %custom-call.14 = f32[1,128,128]{1,2,0:T(8,128)S(1)} custom-call(f32[1,128,128]{2,1,0:T(8,128)S(1)} %get-tuple-element.31), custom_call_target="InvertDiagBlocksLowerTriangular" | custom-call | tf_op jit(solution)/shard_map/jit(cholesky)/cholesky | solution.py:172
  202.7 11.9 %cholesky.105 = f32[128,128]{1,0:T(8,128)S(1)} custom-call(f32[128,128]{1,0:T(8,128)S(1)} %slice_subtract_fusion.2), custom_call_target="Cholesky" | custom-call | tf_op jit(solution)/shard_map/jit(cholesky)/cholesky | solution.py:172
  216.6 3.9 %while.1 = (s32[]{:T(128)}, f32[256,256]{1,0:T(8,128)S(1)}, s32[2,2]{1,0:T(2,128)S(1)}, f32[2,128,128]{2,1,0:T(8,128)S(1)}, s32[]{:T(128)}) while((s32[]{:T(128)}, f32[256,256]{1,0:T(8,128)S(1)}, s32[2,2]{1,0:T(2,128)S(1)}, f32[2,128,128]{2,1,0:T(8,128)S(1)}, s32[]{:T(128)}) %tuple.32), condition=%wide.while_cond, body=%wide.while_body.sunk | while | flops 2 | bytes 131189 | solution.py:173
  217.2 1.3 bitcast_dynamic-update-slice_fusion.2
  219.2 1.3 bitcast_dynamic-update-slice_fusion.2
  220.5 19.7 %custom-call.15 = f32[2,128,128]{1,2,0:T(8,128)S(1)} custom-call(f32[2,128,128]{2,1,0:T(8,128)S(1)} %get-tuple-element.9), custom_call_target="InvertDiagBlocksLowerTriangular" | custom-call | tf_op jit(solution)/shard_map/triangular_solve | solution.py:173
  241.3 1.8 fusion.5
  245.4 31.8 %project_terms.1 = bf16[64,256,128]{2,1,0:T(8,128)(2,1)} custom-call(s32[16]{0:T(128)} %bitcast.52, s32[16,32]{1,0:T(8,128)} %entry_ref.3, bf16[16,32,128,128]{3,2,1,0:T(8,128)(2,1)} %blocks_ref.3, bf16[256,2048]{1,0:T(8,128)(2,1)} %get-tuple-element.26.basis_ref), custom_call_target="tpu_custom_call" | custom-call | tf_op jit(solution)/shard_map/project_terms/pallas_call | solution.py:96
  277.2 9.3 %all-to-all-start.2 = ((bf16[16,4,256,128]{3,2,1,0:T(8,128)(2,1)}), bf16[16,4,256,128]{3,2,1,0:T(8,128)(2,1)}, u32[]{:S(2)}, u32[]{:S(2)}) async-start(bf16[16,4,256,128]{3,2,1,0:T(8,128)(2,1)} %bitcast.48), calls=%async_computation.2 | async-start | bytes 8388608 | tf_op jit(solution)/shard_map/all_to_all | solution.py:178
  288.3 1.3 copy.26
  289.6 90.3 %all-to-all-done.2 = bf16[16,4,256,128]{3,2,1,0:T(8,128)(2,1)} async-done(((bf16[16,4,256,128]{3,2,1,0:T(8,128)(2,1)}), bf16[16,4,256,128]{3,2,1,0:T(8,128)(2,1)}, u32[]{:S(2)}, u32[]{:S(2)}) %all-to-all-start.2) | async-done | bytes 4194336 | tf_op jit(solution)/shard_map/all_to_all | solution.py:178
  379.9 6.8 %owner_sum.1 = bf16[256,8192]{1,0:T(8,128)(2,1)} custom-call(s32[64]{0:T(128)} %reshape.75.goal_ref, bf16[64,256,128]{2,1,0:T(8,128)(2,1)} %bitcast.14.incoming_ref), custom_call_target="tpu_custom_call" | custom-call | tf_op jit(solution)/shard_map/owner_sum/pallas_call | solution.py:131
  (44 shorter events, 11.6 us)
Async XLA Ops:
  136.9 4.4 %collective-permute-start = (f32[2048,256]{1,0:T(8,128)}, f32[2048,256]{1,0:T(8,128)S(1)}, u32[]{:S(2)}, u32[]{:S(2)}) collective-permute-start(f32[2048,256]{1,0:T(8,128)} %sketch_terms.1), channel_id=1, source_target_pairs={{0,1},{1,0},{2,3},{3,2},{4,5},{5,4},{6,7},{7,6},{8,9},{9,8},{10,11... | collective-permute-start | bytes 6291464 | tf_op jit(solution)/shard_map/ppermute | solution.py:170
  141.3 6.6 %copy-start.1 = (f32[2048,256]{1,0:T(8,128)}, f32[2048,256]{1,0:T(8,128)S(1)}, u32[]{:S(2)}) copy-start(f32[2048,256]{1,0:T(8,128)S(1)} %collective-permute-done) | copy-start | bytes 6291460
  147.9 23.7 %copy-start = (f32[2048,256]{1,0:T(8,128)S(1)}, f32[2048,256]{1,0:T(8,128)}, u32[]{:S(2)}) copy-start(f32[2048,256]{1,0:T(8,128)} %sketch_terms.1) | copy-start | bytes 6291460
  147.9 8.4 %collective-permute-start.1 = (f32[256,256]{0,1:T(8,128)S(1)}, f32[256,256]{0,1:T(8,128)S(1)}, u32[]{:S(2)}, u32[]{:S(2)}) collective-permute-start(f32[256,256]{0,1:T(8,128)S(1)} %fusion.2), channel_id=1, source_target_pairs={{0,2},{2,0},{4,6},{6,4},{8,10},{10,8},{12,14},{14,12},{16,18},{18,... | collective-permute-start | bytes 786440 | tf_op jit(solution)/shard_map/ppermute | solution.py:149
  156.3 7.6 %collective-permute-start.2 = (f32[256,256]{0,1:T(8,128)S(1)}, f32[256,256]{0,1:T(8,128)S(1)}, u32[]{:S(2)}, u32[]{:S(2)}) collective-permute-start(f32[256,256]{0,1:T(8,128)S(1)} %add.53), channel_id=1, source_target_pairs={{0,4},{2,6},{4,0},{6,2},{8,12},{10,14},{12,8},{14,10},{16,20},{18,... | collective-permute-start | bytes 786440 | tf_op jit(solution)/shard_map/ppermute | solution.py:149
  163.9 6.8 %collective-permute-start.3 = (f32[256,256]{0,1:T(8,128)S(1)}, f32[256,256]{0,1:T(8,128)S(1)}, u32[]{:S(2)}, u32[]{:S(2)}) collective-permute-start(f32[256,256]{0,1:T(8,128)S(1)} %add.54), channel_id=1, source_target_pairs={{0,8},{2,10},{4,12},{6,14},{8,0},{10,2},{12,4},{14,6},{16,24},{18,... | collective-permute-start | bytes 786440 | tf_op jit(solution)/shard_map/ppermute | solution.py:149
  170.7 9.6 %collective-permute-start.4 = (f32[256,256]{0,1:T(8,128)S(1)}, f32[256,256]{0,1:T(8,128)S(1)}, u32[]{:S(2)}, u32[]{:S(2)}) collective-permute-start(f32[256,256]{0,1:T(8,128)S(1)} %add.55), channel_id=1, source_target_pairs={{0,16},{2,18},{4,20},{6,22},{8,24},{10,26},{12,28},{14,30},{16,0},... | collective-permute-start | bytes 786440 | tf_op jit(solution)/shard_map/ppermute | solution.py:149
  180.4 59.8 %copy-start.2 = (f32[256,2048]{0,1:T(8,128)S(1)}, f32[256,2048]{0,1:T(8,128)}, u32[]{:S(2)}) copy-start(f32[256,2048]{0,1:T(8,128)} %add_bitcast_fusion) | copy-start | bytes 6291460
  277.2 102.7 %all-to-all-start.2 = ((bf16[16,4,256,128]{3,2,1,0:T(8,128)(2,1)}), bf16[16,4,256,128]{3,2,1,0:T(8,128)(2,1)}, u32[]{:S(2)}, u32[]{:S(2)}) async-start(bf16[16,4,256,128]{3,2,1,0:T(8,128)(2,1)} %bitcast.48), calls=%async_computation.2 | async-start | bytes 8388608 | tf_op jit(solution)/shard_map/all_to_all | solution.py:178

commit v2 on v1

--- a/solution.py
+++ b/solution.py
@@ -1,5 +1,3 @@
-import functools
-
 import jax
 import jax.numpy as jnp
 from jax import lax
@@ -142,13 +140,186 @@
     )(goal, incoming)
 
 
-def docs_sum(value):
+MESH = pl.DeviceIdType.MESH
+
+
+def greet_docs():
+    owners, me, core = lax.axis_size("docs"), lax.axis_index("docs"), lax.axis_index("cols")
+    barrier = pltpu.get_barrier_semaphore()
+
+    @pl.loop(1, owners)
+    def _(k):
+        peer = lax.rem(me + k, owners)
+        pl.semaphore_signal(barrier, inc=1, device_id=(peer, core), device_id_type=MESH)
+
+    pl.semaphore_wait(barrier, owners - 1)
+
+
+def exchange_kernel(x_ref, out_ref, send_sem, recv_sem, own_sem):
+    owners, me, core = lax.axis_size("docs"), lax.axis_index("docs"), lax.axis_index("cols")
+    greet_docs()
+
+    def transfer(k):
+        peer = lax.rem(me + k, owners)
+        return pltpu.make_async_remote_copy(
+            src_ref=x_ref.at[peer], dst_ref=out_ref.at[me],
+            send_sem=send_sem.at[k], recv_sem=recv_sem.at[k],
+            device_id=(peer, core), device_id_type=MESH,
+        )
+
+    @pl.loop(1, owners)
+    def _(k):
+        transfer(k).start()
+
+    own = pltpu.make_async_copy(x_ref.at[me], out_ref.at[me], own_sem)
+    own.start()
+    own.wait()
+
+    @pl.loop(1, owners)
+    def _(k):
+        transfer(k).wait()
+
+
+def exchange(value, collective_id, space, name):
     owners = lax.axis_size("docs")
-    step = 1
-    while step < owners:
-        value = value + lax.ppermute(value, "docs", [(i, i ^ step) for i in range(owners)])
-        step *= 2
-    return value
+    return pl.pallas_call(
+        exchange_kernel,
+        out_shape=jax.ShapeDtypeStruct(value.shape, value.dtype),
+        in_specs=[pl.BlockSpec(memory_space=space)],
+        out_specs=pl.BlockSpec(memory_space=space),
+        scratch_shapes=[
+            pltpu.SemaphoreType.DMA((owners,)),
+            pltpu.SemaphoreType.DMA((owners,)),
+            pltpu.SemaphoreType.DMA,
+        ],
+        compiler_params=pltpu.CompilerParams(collective_id=collective_id, has_side_effects=True),
+        name=name,
+    )(value)
+
+
+def gram_sum_kernel(x_ref, out_ref, arrived, send_sem, recv_sem, send_all, recv_all):
+    owners, cores = lax.axis_size("docs"), lax.axis_size("cols")
+    me, core = lax.axis_index("docs"), lax.axis_index("cols")
+    ranks = owners * cores
+    rank = me * cores + core
+    barrier = pltpu.get_barrier_semaphore()
+
+    @pl.loop(1, ranks)
+    def _(k):
+        peer = lax.rem(rank + k, ranks)
+        pl.semaphore_signal(
+            barrier, inc=1, device_id=(peer // cores, lax.rem(peer, cores)), device_id_type=MESH
+        )
+
+    pl.semaphore_wait(barrier, ranks - 1)
+
+    def part(k):
+        peer = lax.rem(me + k, owners)
+        return pltpu.make_async_remote_copy(
+            src_ref=x_ref.at[peer * cores + core], dst_ref=arrived.at[k],
+            send_sem=send_sem.at[k], recv_sem=recv_sem.at[k],
+            device_id=(peer, core), device_id_type=MESH,
+        )
+
+    def result(k):
+        peer = lax.rem(rank + k, ranks)
+        return pltpu.make_async_remote_copy(
+            src_ref=out_ref.at[rank], dst_ref=out_ref.at[rank],
+            send_sem=send_all.at[k], recv_sem=recv_all.at[k],
+            device_id=(peer // cores, lax.rem(peer, cores)), device_id_type=MESH,
+        )
+
+    @pl.loop(1, owners)
+    def _(k):
+        part(k).start()
+
+    @pl.loop(1, owners)
+    def _(k):
+        part(k).wait()
+
+    out_ref[rank] = lax.fori_loop(
+        1, owners, lambda k, total: total + arrived[k], x_ref[rank]
+    )
+
+    @pl.loop(1, ranks)
+    def _(k):
+        result(k).start()
+
+    @pl.loop(1, ranks)
+    def _(k):
+        result(k).wait()
+
+
+def gram_sum(gram):
+    owners, ranks = lax.axis_size("docs"), lax.axis_size("docs") * lax.axis_size("cols")
+    lanes = 128
+    parts = gram.reshape(ranks, gram.size // (ranks * lanes), lanes)
+    summed = pl.pallas_call(
+        gram_sum_kernel,
+        out_shape=jax.ShapeDtypeStruct(parts.shape, parts.dtype),
+        in_specs=[pl.BlockSpec(memory_space=pltpu.VMEM)],
+        out_specs=pl.BlockSpec(memory_space=pltpu.VMEM),
+        scratch_shapes=[
+            pltpu.VMEM((owners,) + parts.shape[1:], parts.dtype),
+            pltpu.SemaphoreType.DMA((owners,)),
+            pltpu.SemaphoreType.DMA((owners,)),
+            pltpu.SemaphoreType.DMA((ranks,)),
+            pltpu.SemaphoreType.DMA((ranks,)),
+        ],
+        compiler_params=pltpu.CompilerParams(collective_id=3, has_side_effects=True),
+        name="gram_sum",
+    )(parts)
+    return summed.reshape(gram.shape)
+
+
+PANEL = 32
+
+
+def inverse_factor_kernel(gram_ref, out_ref, work):
+    size = gram_ref.shape[0]
+    work[:, :size] = gram_ref[...]
+    rows = lax.broadcasted_iota(jnp.int32, (size, size), 0)
+    lanes = lax.broadcasted_iota(jnp.int32, (size, size), 1)
+    work[:, size:] = (rows == lanes).astype(jnp.float32)
+    row_at = lax.broadcasted_iota(jnp.int32, (PANEL, 1), 0)
+    for first in range(0, size, PANEL):
+        low = first // 128 * 128
+        high = size + low + 128
+        panel = work[first : first + PANEL, low:high]
+        for j in range(PANEL):
+            at = first - low + j
+            column = panel[:, at : at + 1]
+            pivot = column[j : j + 1]
+            scale = lax.rsqrt(pivot)
+            scale = scale * (1.5 - 0.5 * pivot * scale * scale)
+            row = panel[j : j + 1] * scale
+            factor = jnp.where(row_at > j, column * scale, 0.0)
+            panel = jnp.where(row_at == j, row, panel - factor * row)
+        out_ref[first : first + PANEL, : low + 128] = panel[:, size - low :]
+        if low + 128 < size:
+            out_ref[first : first + PANEL, low + 128 :] = jnp.zeros(
+                (PANEL, size - low - 128), jnp.float32
+            )
+        below = first + PANEL
+        if below < size:
+            upper = panel[:, : size - low]
+            change = lax.dot_general(
+                upper, panel, (((0,), (0,)), ((), ())),
+                precision=lax.Precision.HIGHEST, preferred_element_type=jnp.float32,
+            )
+            work[below:, low:high] -= change[below - low :]
+
+
+def inverse_factor(gram):
+    size = gram.shape[0]
+    return pl.pallas_call(
+        inverse_factor_kernel,
+        out_shape=jax.ShapeDtypeStruct(gram.shape, jnp.float32),
+        in_specs=[pl.BlockSpec(memory_space=pltpu.VMEM)],
+        out_specs=pl.BlockSpec(memory_space=pltpu.VMEM),
+        scratch_shapes=[pltpu.VMEM((size, 2 * size), jnp.float32)],
+        name="inverse_factor",
+    )(gram)
 
 
 def on_device(blocks, slot_entry, ghost_table, live_counts, test_matrix):
@@ -159,25 +330,23 @@
     per_owner = table.shape[1]
     entries = owners * per_owner
     live = live_counts.reshape(block_rows)
-    requests = lax.all_to_all(table, "docs", split_axis=0, concat_axis=0, tiled=True)
+    padded = jnp.pad(table[:, None, :], ((0, 0), (0, 0), (0, 128 - per_owner)))
+    requests = exchange(padded, 0, pltpu.VMEM, "requests")[:, 0, :per_owner]
     local_pieces = test_matrix.reshape(-1, block_edge, sketch_width)
-    fetched = lax.all_to_all(
-        local_pieces[requests], "docs", split_axis=0, concat_axis=0, tiled=True
-    )
+    fetched = exchange(local_pieces[requests], 1, pl.ANY, "fetch")
     fetched = fetched.reshape(entries, block_edge, sketch_width)
 
     terms = sketch_terms(live, slot_entry, blocks, fetched)
     sketch = terms + lax.ppermute(terms, "cols", [(0, 1), (1, 0)])
-    gram = docs_sum(gram_of(sketch))
-    lower = jnp.linalg.cholesky(gram)
-    basis = lax.linalg.triangular_solve(lower, sketch.T, left_side=True, lower=True)
-    basis = basis.astype(jnp.bfloat16)
-    basis_rows = basis.T
+    inverse = inverse_factor(gram_sum(gram_of(sketch)))
+    basis_rows = lax.dot_general(
+        sketch, inverse, (((1,), (1,)), ((), ())), precision=lax.Precision.HIGHEST
+    ).astype(jnp.bfloat16)
+    basis = basis_rows.T
 
     outgoing = project_terms(live, slot_entry, blocks, basis, entries)
-    incoming = lax.all_to_all(
-        outgoing.reshape(owners, per_owner, sketch_width, block_edge),
-        "docs", split_axis=0, concat_axis=0, tiled=True,
+    incoming = exchange(
+        outgoing.reshape(owners, per_owner, sketch_width, block_edge), 2, pl.ANY, "giveback"
     )
     projected = owner_sum(
         requests.reshape(-1),

time: 389 us -> 359 us (0.923)
  Pallas kernels: 59.5 us -> 332 us
  waiting for transfers between devices: 121 us -> 3.5 us
  blocking collectives: 109 us -> 0 us
  other arithmetic: 59.1 us -> 2.5 us
  starting transfers between devices: 11.8 us -> 0.9 us
  matrix products: 11 us -> 6.44 us
    pallas_call x0 -> x5, Pallas kernels: none -> 273 us  [the longest x3 229 us: exchange(): pl.pallas_call(exchange_kernel, out_shape=jax.ShapeDtypeStruct(value.shap...]
    all_to_all x2 -> x0, blocking collectives: 109 us -> none  [the longest x1 98.2 us: on_device(): lax.all_to_all(local_pieces[requests], 'docs', split_axis=0, concat_axis=...]
    all_to_all x1 -> x0, waiting for transfers between devices: 90.3 us -> none  [on_device(): lax.all_to_all(outgoing.reshape(owners, per_owner, sketch_width, block_ed...]
    another operation x10 -> x0, other arithmetic: 55.1 us -> none  [the longest x6 34.2 us: on_device(): lower = jnp.linalg.cholesky(gram)]
    ppermute x4 -> x0, waiting for transfers between devices: 26.6 us -> none  [docs_sum(): lax.ppermute(value, 'docs', [(i, i ^ step) for i in range(owners)])]
    all_to_all x1 -> x0, starting transfers between devices: 9.3 us -> none  [on_device(): lax.all_to_all(outgoing.reshape(owners, per_owner, sketch_width, block_ed...]
    another operation x5 -> x0, matrix products: 4.42 us -> none  [the longest x3 3.95 us: on_device(): lax.linalg.triangular_solve(lower, sketch.T, left_side=True, lower=True)]
  transfers between devices with their start and end apart: 6 -> 1, of which waited for: 6 -> 1; matrix products, arithmetic and copies ran while one was open for 2% -> 0% of each run, Pallas kernels for 0% -> 0%
where the time goes in v2:
time: 359 us; the launch traced here: 357 us
  Pallas kernels  332 us (92%)
  local copies, waits for them, and re-layouts  11.8 us (3%)
  matrix products  6.44 us (2%)
    pallas_call x3, Pallas kernels, exchange(): pl.pallas_call(exchange_kernel, out_shape=jax.ShapeDtypeStruct(value.shap...  229 us
    pallas_call x1, Pallas kernels, project_terms(): pl.pallas_call(project_kernel, out_shape=jax.ShapeDtypeStruct((entries, w...  30.9 us
    pallas_call x1, Pallas kernels, inverse_factor(): pl.pallas_call(inverse_factor_kernel, out_shape=jax.ShapeDtypeStruct(gram...  27.6 us
    pallas_call x1, Pallas kernels, sketch_terms(): pl.pallas_call(sketch_kernel, out_shape=jax.ShapeDtypeStruct((block_rows...  20.6 us
    pallas_call x1, Pallas kernels, gram_sum(): pl.pallas_call(gram_sum_kernel, out_shape=jax.ShapeDtypeStruct(parts.shap...  17.1 us
  transfers between devices with their start and end apart: 1, of which 1 were waited for; matrix products, arithmetic and copies ran while one was open for 0% of the time, Pallas kernels for 0%

profile of v2, /device:TPU:14, one launch (start us, length us, event | category | flops | bytes accessed | tf_op | source)
XLA Modules:
  0.0 357.4 jit_solution(6058327237145675986)
XLA Ops:
  0.6 0.8 copy.12
  1.4 0.6 pad.4.x_ref
  2.0 9.0 %requests.1 = s32[16,1,128]{2,1,0:T(1,128)} custom-call(s32[16,1,128]{2,1,0:T(1,128)} %pad.4.x_ref), custom_call_target="tpu_custom_call" | custom-call | tf_op jit(solution)/shard_map/requests/pallas_call | solution.py:185
  11.0 0.7 slice_reduce_fusion
  11.7 0.1 copy.13
  11.8 0.1 copy.14
  11.9 0.1 reshape.62
  12.0 5.0 %gather_fusion = bf16[64,128,256]{2,1,0:T(8,128)(2,1)} fusion(bf16[64,128,256]{2,1,0:T(8,128)(2,1)} %bitcast.21, s32[1024]{0:T(1024)S(1)} %pad_clamp_fusion), kind=kCustom, calls=%fused_computation | custom fusion | bytes 8388864 | tf_op jit(solution)/shard_map/gather | solution.py:336
  17.0 104.5 %fetch.1 = bf16[16,4,128,256]{3,2,1,0:T(8,128)(2,1)} custom-call(bf16[16,4,128,256]{3,2,1,0:T(8,128)(2,1)} %bitcast.16), custom_call_target="tpu_custom_call" | custom-call | tf_op jit(solution)/shard_map/fetch/pallas_call | solution.py:185
  121.5 20.6 %sketch_terms.1 = f32[2048,256]{1,0:T(8,128)} custom-call(s32[16]{0:T(128)} %bitcast.22, s32[16,32]{1,0:T(8,128)} %entry_ref.3, bf16[16,32,128,128]{3,2,1,0:T(8,128)(2,1)} %blocks_ref.3, bf16[64,128,256]{2,1,0:T(8,128)(2,1)} %bitcast.18), custom_call_target="tpu_custom_call" | custom-call | tf_op jit(solution)/shard_map/sketch_terms/pallas_call | solution.py:43
  142.1 0.9 collective-permute-start
  143.0 0.6 reshape_squeeze.3.goal_ref
  143.6 3.5 collective-permute-done
  147.1 2.5 add.20
  149.6 3.5 fusion
  153.1 0.7 reshape.56.x_ref
  153.8 17.1 %gram_sum.1 = f32[32,16,128]{2,1,0:T(8,128)} custom-call(f32[32,16,128]{2,1,0:T(8,128)} %reshape.56.x_ref), custom_call_target="tpu_custom_call" | custom-call | tf_op jit(solution)/shard_map/gram_sum/pallas_call | solution.py:257
  171.0 1.7 reshape.57.gram_ref
  172.7 27.6 %inverse_factor.1 = f32[256,256]{1,0:T(8,128)} custom-call(f32[256,256]{1,0:T(8,128)} %reshape.57.gram_ref), custom_call_target="tpu_custom_call" | custom-call | tf_op jit(solution)/shard_map/inverse_factor/pallas_call | solution.py:315
  200.3 3.0 convolution_convert_fusion
  203.3 1.3 copy.16
  204.6 30.9 %project_terms.1 = bf16[64,256,128]{2,1,0:T(8,128)(2,1)} custom-call(s32[16]{0:T(128)} %bitcast.23, s32[16,32]{1,0:T(8,128)} %entry_ref.3, bf16[16,32,128,128]{3,2,1,0:T(8,128)(2,1)} %blocks_ref.3, bf16[256,2048]{1,0:T(8,128)(2,1)} %bitcast.20), custom_call_target="tpu_custom_call" | custom-call | tf_op jit(solution)/shard_map/project_terms/pallas_call | solution.py:94
  235.5 115.1 %giveback.1 = bf16[16,4,256,128]{3,2,1,0:T(8,128)(2,1)} custom-call(bf16[16,4,256,128]{3,2,1,0:T(8,128)(2,1)} %bitcast.19), custom_call_target="tpu_custom_call" | custom-call | tf_op jit(solution)/shard_map/giveback/pallas_call | solution.py:185
  350.6 6.8 %owner_sum.1 = bf16[256,8192]{1,0:T(8,128)(2,1)} custom-call(s32[64]{0:T(128)} %reshape_squeeze.3.goal_ref, bf16[64,256,128]{2,1,0:T(8,128)(2,1)} %bitcast.17), custom_call_target="tpu_custom_call" | custom-call | tf_op jit(solution)/shard_map/owner_sum/pallas_call | solution.py:129
  (4 shorter events, 0.0 us)
Async XLA Ops:
  142.1 5.0 %collective-permute-start = (f32[2048,256]{1,0:T(8,128)}, f32[2048,256]{1,0:T(8,128)}, u32[]{:S(2)}, u32[]{:S(2)}) collective-permute-start(f32[2048,256]{1,0:T(8,128)} %sketch_terms.1), channel_id=1, source_target_pairs={{0,1},{1,0},{2,3},{3,2},{4,5},{5,4},{6,7},{7,6},{8,9},{9,8},{10,11... | collective-permute-start | bytes 6291464 | tf_op jit(solution)/shard_map/ppermute | solution.py:340
  203.3 1.3 copy-start

commit v3 on v2

--- a/solution.py
+++ b/solution.py
@@ -6,126 +6,93 @@
 from jax.sharding import PartitionSpec as P
 
 VMEM_BYTES = 60 * 1024 * 1024
-SKETCH_GROUP = 8
-PROJECT_GROUP = 4
-
-
 def gram_of(rows_block):
     return lax.dot_general(
         rows_block, rows_block, (((0,), (0,)), ((), ())), precision=lax.Precision.HIGHEST
     )
 
 
-def live_block(blocks_ref, k, live):
-    stored = blocks_ref[0, k]
-    return jnp.where(k < live, stored, jnp.zeros_like(stored))
-
-
-def sketch_kernel(live_ref, entry_ref, blocks_ref, fetched_ref, out_ref):
+def place_kernel(live_ref, entry_ref, blocks_ref, out_ref):
     row = pl.program_id(0)
-    live = live_ref[row]
-    out_ref[...] = jnp.zeros_like(out_ref)
-
-    def body(group, carry):
-        first = group * SKETCH_GROUP
-        slots = [first + i for i in range(SKETCH_GROUP)]
-        stored = jnp.concatenate([live_block(blocks_ref, k, live) for k in slots], axis=1)
-        pieces = jnp.concatenate([fetched_ref[entry_ref[row, k]] for k in slots], axis=0)
-        out_ref[...] += jnp.dot(stored, pieces, preferred_element_type=jnp.float32)
-        return carry
-
-    lax.fori_loop(0, (live + SKETCH_GROUP - 1) // SKETCH_GROUP, body, 0)
-
-
-def sketch_terms(live, slot_entry, blocks, fetched):
+    edge = blocks_ref.shape[-1]
+    per_owner = out_ref.shape[-1] // edge
+
+    @pl.loop(0, out_ref.shape[0])
+    def _(o):
+        out_ref[o] = jnp.zeros(out_ref.shape[1:], out_ref.dtype)
+
+    @pl.loop(0, live_ref[row])
+    def _(k):
+        entry = entry_ref[row, k]
+        lane = pl.multiple_of(lax.rem(entry, per_owner) * edge, edge)
+        out_ref[lax.div(entry, per_owner), :, pl.ds(lane, edge)] = blocks_ref[0, k]
+
+
+def place_blocks(live, slot_entry, blocks, owners, per_owner):
     block_rows, slots, edge, _ = blocks.shape
-    width = fetched.shape[-1]
-    return pl.pallas_call(
-        sketch_kernel,
-        out_shape=jax.ShapeDtypeStruct((block_rows * edge, width), jnp.float32),
+    shape = (owners, block_rows * edge, per_owner * edge)
+    return pl.pallas_call(
+        place_kernel,
+        out_shape=jax.ShapeDtypeStruct(shape, blocks.dtype),
         grid_spec=pltpu.PrefetchScalarGridSpec(
             num_scalar_prefetch=2,
             grid=(block_rows,),
-            in_specs=[
-                pl.BlockSpec((1, slots, edge, edge), lambda r, *_: (r, 0, 0, 0)),
-                pl.BlockSpec(memory_space=pltpu.VMEM),
-            ],
-            out_specs=pl.BlockSpec((edge, width), lambda r, *_: (r, 0)),
+            in_specs=[pl.BlockSpec((1, slots, edge, edge), lambda r, *_: (r, 0, 0, 0))],
+            out_specs=pl.BlockSpec((owners, edge, per_owner * edge), lambda r, *_: (0, r, 0)),
         ),
         compiler_params=pltpu.CompilerParams(vmem_limit_bytes=VMEM_BYTES),
+        cost_estimate=pl.CostEstimate(
+            flops=0, transcendentals=0, bytes_accessed=2 * (blocks.size + shape[0] * shape[1] * shape[2])
+        ),
+        name="place_blocks",
+    )(live, slot_entry, blocks)
+
+
+def sketch_kernel(placed_ref, pieces_ref, out_ref):
+    @pl.when(pl.program_id(0) == 0)
+    def _():
+        out_ref[...] = jnp.zeros_like(out_ref)
+
+    out_ref[...] += jnp.dot(placed_ref[0], pieces_ref[0], preferred_element_type=jnp.float32)
+
+
+def sketch_terms(placed, pieces):
+    owners, rows, depth = placed.shape
+    width = pieces.shape[-1]
+    return pl.pallas_call(
+        sketch_kernel,
+        out_shape=jax.ShapeDtypeStruct((rows, width), jnp.float32),
+        grid=(owners,),
+        in_specs=[
+            pl.BlockSpec((1, rows, depth), lambda o: (o, 0, 0)),
+            pl.BlockSpec((1, depth, width), lambda o: (o, 0, 0)),
+        ],
+        out_specs=pl.BlockSpec((rows, width), lambda o: (0, 0)),
+        compiler_params=pltpu.CompilerParams(vmem_limit_bytes=VMEM_BYTES),
         name="sketch_terms",
-    )(live, slot_entry, blocks, fetched)
-
-
-def project_kernel(live_ref, entry_ref, blocks_ref, basis_ref, out_ref, total):
-    row = pl.program_id(0)
-    edge = blocks_ref.shape[-1]
-    live = live_ref[row]
-
-    @pl.when(row == 0)
-    def _():
-        @pl.loop(0, total.shape[0])
-        def _(e):
-            total[e] = jnp.zeros(total.shape[1:], total.dtype)
-
-    basis = basis_ref[...]
-
-    def body(group, carry):
-        first = group * PROJECT_GROUP
-        slots = [first + i for i in range(PROJECT_GROUP)]
-        stored = jnp.concatenate([live_block(blocks_ref, k, live) for k in slots], axis=1)
-        terms = jnp.dot(basis, stored, preferred_element_type=jnp.float32)
-        for i, k in enumerate(slots):
-            total[entry_ref[row, k]] += terms[:, i * edge : (i + 1) * edge]
-        return carry
-
-    lax.fori_loop(0, (live + PROJECT_GROUP - 1) // PROJECT_GROUP, body, 0)
-
-    @pl.when(row == pl.num_programs(0) - 1)
-    def _():
-        @pl.loop(0, total.shape[0])
-        def _(e):
-            out_ref[e] = total[e].astype(out_ref.dtype)
-
-
-def project_terms(live, slot_entry, blocks, basis, entries):
-    block_rows, slots, edge, _ = blocks.shape
-    width = basis.shape[0]
-    return pl.pallas_call(
-        project_kernel,
-        out_shape=jax.ShapeDtypeStruct((entries, width, edge), jnp.bfloat16),
-        grid_spec=pltpu.PrefetchScalarGridSpec(
-            num_scalar_prefetch=2,
-            grid=(block_rows,),
-            in_specs=[
-                pl.BlockSpec((1, slots, edge, edge), lambda r, *_: (r, 0, 0, 0)),
-                pl.BlockSpec((width, edge), lambda r, *_: (0, r)),
-            ],
-            out_specs=pl.BlockSpec(memory_space=pltpu.VMEM),
-            scratch_shapes=[pltpu.VMEM((entries, width, edge), jnp.float32)],
-        ),
-        compiler_params=pltpu.CompilerParams(vmem_limit_bytes=VMEM_BYTES),
-        name="project_terms",
-    )(live, slot_entry, blocks, basis)
+    )(placed, pieces)
 
 
 def owner_sum_kernel(goal_ref, incoming_ref, out_ref, total):
-    edge = incoming_ref.shape[-1]
+    edge = total.shape[-1]
+    per_owner = incoming_ref.shape[-1] // edge
 
     @pl.loop(0, total.shape[0])
     def _(b):
         total[b] = jnp.zeros(total.shape[1:], total.dtype)
 
     @pl.loop(0, incoming_ref.shape[0])
-    def _(i):
-        total[goal_ref[i]] += incoming_ref[i].astype(jnp.float32)
+    def _(o):
+        for j in range(per_owner):
+            part = incoming_ref[o, :, j * edge : (j + 1) * edge]
+            total[goal_ref[o * per_owner + j]] += part.astype(jnp.float32)
 
     for b in range(total.shape[0]):
         out_ref[:, b * edge : (b + 1) * edge] = total[b].astype(out_ref.dtype)
 
 
-def owner_sum(goal, incoming, owned_blocks):
-    _, width, edge = incoming.shape
+def owner_sum(goal, incoming, owned_blocks, edge):
+    _, width, _ = incoming.shape
     return pl.pallas_call(
         owner_sum_kernel,
         out_shape=jax.ShapeDtypeStruct((width, owned_blocks * edge), jnp.bfloat16),
@@ -195,6 +162,88 @@
         compiler_params=pltpu.CompilerParams(collective_id=collective_id, has_side_effects=True),
         name=name,
     )(value)
+
+
+def partner(me, k, owners):
+    total, bit = 0, 1
+    while bit < owners:
+        total = total + lax.rem(lax.div(me, bit) + lax.div(k, bit), 2) * bit
+        bit *= 2
+    return total
+
+
+def project_kernel(basis_ref, placed_ref, out_ref, chunk, stage, chunk_sem, send_sem, recv_sem, own_sem):
+    owners, me, core = lax.axis_size("docs"), lax.axis_index("docs"), lax.axis_index("cols")
+    greet_docs()
+
+    def offset(i):
+        return lax.rem(i + owners // 2, owners)
+
+    def load(i):
+        slot = lax.rem(i, 2)
+        peer = partner(me, offset(i), owners)
+        return pltpu.make_async_copy(placed_ref.at[peer], chunk.at[slot], chunk_sem.at[slot])
+
+    def send(k):
+        peer = partner(me, k, owners)
+        return pltpu.make_async_remote_copy(
+            src_ref=stage.at[peer], dst_ref=out_ref.at[me],
+            send_sem=send_sem.at[k], recv_sem=recv_sem.at[k],
+            device_id=(peer, core), device_id_type=MESH,
+        )
+
+    own = pltpu.make_async_copy(stage.at[me], out_ref.at[me], own_sem)
+    load(jnp.int32(0)).start()
+
+    @pl.loop(0, owners)
+    def _(i):
+        @pl.when(i + 1 < owners)
+        def _():
+            load(i + 1).start()
+
+        load(i).wait()
+        k = offset(i)
+        stage[partner(me, k, owners)] = jnp.dot(
+            basis_ref[...], chunk[lax.rem(i, 2)], preferred_element_type=jnp.float32
+        ).astype(stage.dtype)
+
+        @pl.when(k != 0)
+        def _():
+            send(k).start()
+
+        @pl.when(k == 0)
+        def _():
+            own.start()
+
+    own.wait()
+
+    @pl.loop(1, owners)
+    def _(k):
+        send(k).wait()
+
+
+def project_terms(basis, placed):
+    owners, rows, depth = placed.shape
+    width = basis.shape[0]
+    shape = (owners, width, depth)
+    return pl.pallas_call(
+        project_kernel,
+        out_shape=jax.ShapeDtypeStruct(shape, jnp.bfloat16),
+        in_specs=[pl.BlockSpec(memory_space=pltpu.VMEM), pl.BlockSpec(memory_space=pl.ANY)],
+        out_specs=pl.BlockSpec(memory_space=pl.ANY),
+        scratch_shapes=[
+            pltpu.VMEM((2, rows, depth), jnp.bfloat16),
+            pltpu.VMEM(shape, jnp.bfloat16),
+            pltpu.SemaphoreType.DMA((2,)),
+            pltpu.SemaphoreType.DMA((owners,)),
+            pltpu.SemaphoreType.DMA((owners,)),
+            pltpu.SemaphoreType.DMA,
+        ],
+        compiler_params=pltpu.CompilerParams(
+            collective_id=2, has_side_effects=True, vmem_limit_bytes=VMEM_BYTES
+        ),
+        name="project_terms",
+    )(basis, placed)
 
 
 def gram_sum_kernel(x_ref, out_ref, arrived, send_sem, recv_sem, send_all, recv_all):
@@ -328,15 +377,17 @@
     owners = lax.axis_size("docs")
     table = ghost_table.reshape(owners, ghost_table.shape[-1])
     per_owner = table.shape[1]
-    entries = owners * per_owner
     live = live_counts.reshape(block_rows)
     padded = jnp.pad(table[:, None, :], ((0, 0), (0, 0), (0, 128 - per_owner)))
     requests = exchange(padded, 0, pltpu.VMEM, "requests")[:, 0, :per_owner]
     local_pieces = test_matrix.reshape(-1, block_edge, sketch_width)
-    fetched = exchange(local_pieces[requests], 1, pl.ANY, "fetch")
-    fetched = fetched.reshape(entries, block_edge, sketch_width)
-
-    terms = sketch_terms(live, slot_entry, blocks, fetched)
+    fetched = lax.all_to_all(
+        local_pieces[requests], "docs", split_axis=0, concat_axis=0, tiled=True
+    )
+    pieces = fetched.reshape(owners, per_owner * block_edge, sketch_width)
+    placed = place_blocks(live, slot_entry, blocks, owners, per_owner)
+
+    terms = sketch_terms(placed, pieces)
     sketch = terms + lax.ppermute(terms, "cols", [(0, 1), (1, 0)])
     inverse = inverse_factor(gram_sum(gram_of(sketch)))
     basis_rows = lax.dot_general(
@@ -344,14 +395,9 @@
     ).astype(jnp.bfloat16)
     basis = basis_rows.T
 
-    outgoing = project_terms(live, slot_entry, blocks, basis, entries)
-    incoming = exchange(
-        outgoing.reshape(owners, per_owner, sketch_width, block_edge), 2, pl.ANY, "giveback"
-    )
+    incoming = project_terms(basis, placed)
     projected = owner_sum(
-        requests.reshape(-1),
-        incoming.reshape(-1, sketch_width, block_edge),
-        test_matrix.shape[0] // block_edge,
+        requests.reshape(-1), incoming, test_matrix.shape[0] // block_edge, block_edge
     )
     return (basis_rows, projected)
 

time: 359 us -> 308 us (0.86)
  Pallas kernels: 332 us -> 204 us
  waiting for transfers between devices: 3.5 us -> 73.1 us
  starting transfers between devices: 0.9 us -> 6.92 us
    pallas_call x3 -> x1, Pallas kernels: 229 us -> 9 us  [exchange(): pl.pallas_call(exchange_kernel, out_shape=jax.ShapeDtypeStruct(value.shap...]
    pallas_call x2 -> x3, Pallas kernels: 51.4 us -> 143 us  [the longest x1 98.5 us: project_terms(): pl.pallas_call(project_kernel, out_shape=jax.ShapeDtypeStruct(shape, jnp....]
    all_to_all x0 -> x1, waiting for transfers between devices: none -> 69.2 us  [on_device(): lax.all_to_all(local_pieces[requests], 'docs', split_axis=0, concat_axis=...]
    all_to_all x0 -> x1, starting transfers between devices: none -> 6.92 us  [on_device(): lax.all_to_all(local_pieces[requests], 'docs', split_axis=0, concat_axis=...]
  transfers between devices with their start and end apart: 1 -> 2, of which waited for: 1 -> 2; matrix products, arithmetic and copies ran while one was open for 0% -> 0% of each run, Pallas kernels for 0% -> 8%
where the time goes in v3:
time: 308 us; the launch traced here: 305 us
  Pallas kernels  204 us (66%)
  waiting for transfers between devices  73.1 us (24%)
  local copies, waits for them, and re-layouts  11.8 us (4%)
  starting transfers between devices  6.92 us (2%)
  matrix products  6.44 us (2%)
    pallas_call x1, Pallas kernels, project_terms(): pl.pallas_call(project_kernel, out_shape=jax.ShapeDtypeStruct(shape, jnp....  98.5 us
    all_to_all x1, waiting for transfers between devices, on_device(): lax.all_to_all(local_pieces[requests], 'docs', split_axis=0, concat_axis=...  69.2 us
    pallas_call x1, Pallas kernels, inverse_factor(): pl.pallas_call(inverse_factor_kernel, out_shape=jax.ShapeDtypeStruct(gram...  27.6 us
    pallas_call x1, Pallas kernels, place_blocks(): pl.pallas_call(place_kernel, out_shape=jax.ShapeDtypeStruct(shape, blocks...  22.9 us
    pallas_call x1, Pallas kernels, sketch_terms(): pl.pallas_call(sketch_kernel, out_shape=jax.ShapeDtypeStruct((rows, width...  21.8 us
    pallas_call x1, Pallas kernels, gram_sum(): pl.pallas_call(gram_sum_kernel, out_shape=jax.ShapeDtypeStruct(parts.shap...  17.2 us
    pallas_call x1, Pallas kernels, exchange(): pl.pallas_call(exchange_kernel, out_shape=jax.ShapeDtypeStruct(value.shap...  9 us
    all_to_all x1, starting transfers between devices, on_device(): lax.all_to_all(local_pieces[requests], 'docs', split_axis=0, concat_axis=...  6.92 us
  transfers between devices with their start and end apart: 2, of which 2 were waited for; matrix products, arithmetic and copies ran while one was open for 0% of the time, Pallas kernels for 8%

profile of v3, /device:TPU:14, one launch (start us, length us, event | category | flops | bytes accessed | tf_op | source)
XLA Modules:
  0.0 305.3 jit_solution(5243780199786524563)
XLA Ops:
  0.6 0.8 copy.12
  1.4 0.6 pad.4.x_ref
  2.0 9.0 %requests.1 = s32[16,1,128]{2,1,0:T(1,128)} custom-call(s32[16,1,128]{2,1,0:T(1,128)} %pad.4.x_ref), custom_call_target="tpu_custom_call" | custom-call | tf_op jit(solution)/shard_map/requests/pallas_call | solution.py:152
  11.0 0.7 slice_reduce_fusion
  11.7 0.1 copy.13
  11.8 0.1 copy.14
  11.9 0.1 reshape.54
  12.0 5.0 %gather_fusion = bf16[64,128,256]{2,1,0:T(8,128)(2,1)} fusion(bf16[64,128,256]{2,1,0:T(8,128)(2,1)} %bitcast.16, s32[1024]{0:T(1024)S(1)} %pad_clamp_fusion), kind=kCustom, calls=%fused_computation | custom fusion | bytes 8388864 | tf_op jit(solution)/shard_map/gather | solution.py:385
  17.0 6.9 %all-to-all-start = ((bf16[16,4,128,256]{3,2,1,0:T(8,128)(2,1)}), bf16[16,4,128,256]{3,2,1,0:T(8,128)(2,1)}, u32[]{:S(2)}, u32[]{:S(2)}) async-start(bf16[16,4,128,256]{3,2,1,0:T(8,128)(2,1)} %bitcast.14), calls=%async_computation | async-start | bytes 8388608 | tf_op jit(solution)/shard_map/all_to_all | solution.py:384
  24.0 22.9 %place_blocks.1.placed_ref = bf16[16,2048,512]{2,1,0:T(8,128)(2,1)} custom-call(s32[16]{0:T(128)} %bitcast.18, s32[16,32]{1,0:T(8,128)} %entry_ref.1, bf16[16,32,128,128]{3,2,1,0:T(8,128)(2,1)} %blocks_ref.1), custom_call_target="tpu_custom_call" | custom-call | bytes 50331648 | tf_op jit(solution)/shard_map/place_blocks/pallas_call | solution.py:34
  46.9 69.2 %all-to-all-done = bf16[16,4,128,256]{3,2,1,0:T(8,128)(2,1)} async-done(((bf16[16,4,128,256]{3,2,1,0:T(8,128)(2,1)}), bf16[16,4,128,256]{3,2,1,0:T(8,128)(2,1)}, u32[]{:S(2)}, u32[]{:S(2)}) %all-to-all-start) | async-done | bytes 4194336 | tf_op jit(solution)/shard_map/all_to_all | solution.py:384
  116.1 21.8 %sketch_terms.1 = f32[2048,256]{1,0:T(8,128)} custom-call(bf16[16,2048,512]{2,1,0:T(8,128)(2,1)} %place_blocks.1.placed_ref, bf16[16,512,256]{2,1,0:T(8,128)(2,1)} %bitcast.5.pieces_ref), custom_call_target="tpu_custom_call" | custom-call | tf_op jit(solution)/shard_map/sketch_terms/pallas_call | solution.py:62
  137.9 0.6 reshape_squeeze.3.goal_ref
  138.5 3.9 %collective-permute-done = f32[2048,256]{1,0:T(8,128)} collective-permute-done((f32[2048,256]{1,0:T(8,128)}, f32[2048,256]{1,0:T(8,128)}, u32[]{:S(2)}, u32[]{:S(2)}) %collective-permute-start) | collective-permute-done | bytes 2097184 | tf_op jit(solution)/shard_map/ppermute | solution.py:391
  142.4 2.5 add.20
  144.9 3.5 %fusion = f32[256,256]{1,0:T(8,128)S(1)} fusion(f32[2048,256]{1,0:T(8,128)S(1)} %add.20), kind=kOutput, calls=%fused_computation.5 | convolution fusion | flops 1610612736 | bytes 2359296 | tf_op jit(solution)/shard_map/dot_general | solution.py:10
  148.4 0.7 reshape.50.x_ref
  149.1 17.2 %gram_sum.1 = f32[32,16,128]{2,1,0:T(8,128)} custom-call(f32[32,16,128]{2,1,0:T(8,128)} %reshape.50.x_ref), custom_call_target="tpu_custom_call" | custom-call | tf_op jit(solution)/shard_map/gram_sum/pallas_call | solution.py:306
  166.3 1.7 reshape.51.gram_ref
  168.0 27.6 %inverse_factor.1 = f32[256,256]{1,0:T(8,128)} custom-call(f32[256,256]{1,0:T(8,128)} %reshape.51.gram_ref), custom_call_target="tpu_custom_call" | custom-call | tf_op jit(solution)/shard_map/inverse_factor/pallas_call | solution.py:364
  195.7 3.0 convolution_convert_fusion
  198.6 1.4 copy.16
  200.0 98.5 %project_terms.1.incoming_ref = bf16[16,256,512]{2,1,0:T(8,128)(2,1)} custom-call(bf16[256,2048]{1,0:T(8,128)(2,1)} %bitcast.15, bf16[16,2048,512]{2,1,0:T(8,128)(2,1)} %place_blocks.1.placed_ref), custom_call_target="tpu_custom_call" | custom-call | tf_op jit(solution)/shard_map/project_terms/pallas_call | solution.py:229
  298.5 6.8 %owner_sum.1 = bf16[256,8192]{1,0:T(8,128)(2,1)} custom-call(s32[64]{0:T(128)} %reshape_squeeze.3.goal_ref, bf16[16,256,512]{2,1,0:T(8,128)(2,1)} %project_terms.1.incoming_ref), custom_call_target="tpu_custom_call" | custom-call | tf_op jit(solution)/shard_map/owner_sum/pallas_call | solution.py:96
  (5 shorter events, 0.0 us)
Async XLA Ops:
  17.0 99.0 %all-to-all-start = ((bf16[16,4,128,256]{3,2,1,0:T(8,128)(2,1)}), bf16[16,4,128,256]{3,2,1,0:T(8,128)(2,1)}, u32[]{:S(2)}, u32[]{:S(2)}) async-start(bf16[16,4,128,256]{3,2,1,0:T(8,128)(2,1)} %bitcast.14), calls=%async_computation | async-start | bytes 8388608 | tf_op jit(solution)/shard_map/all_to_all | solution.py:384
  137.9 4.5 %collective-permute-start = (f32[2048,256]{1,0:T(8,128)}, f32[2048,256]{1,0:T(8,128)}, u32[]{:S(2)}, u32[]{:S(2)}) collective-permute-start(f32[2048,256]{1,0:T(8,128)} %sketch_terms.1), channel_id=1, source_target_pairs={{0,1},{1,0},{2,3},{3,2},{4,5},{5,4},{6,7},{7,6},{8,9},{9,8},{10,11... | collective-permute-start | bytes 6291464 | tf_op jit(solution)/shard_map/ppermute | solution.py:391
  198.6 1.4 copy-start

commit v4 on v3

--- a/solution.py
+++ b/solution.py
@@ -6,6 +6,7 @@
 from jax.sharding import PartitionSpec as P
 
 VMEM_BYTES = 60 * 1024 * 1024
+SKETCH_ROWS = 256
 def gram_of(rows_block):
     return lax.dot_general(
         rows_block, rows_block, (((0,), (0,)), ((), ())), precision=lax.Precision.HIGHEST
@@ -49,11 +50,10 @@
 
 
 def sketch_kernel(placed_ref, pieces_ref, out_ref):
-    @pl.when(pl.program_id(0) == 0)
-    def _():
-        out_ref[...] = jnp.zeros_like(out_ref)
-
-    out_ref[...] += jnp.dot(placed_ref[0], pieces_ref[0], preferred_element_type=jnp.float32)
+    out_ref[...] = sum(
+        jnp.dot(placed_ref[o], pieces_ref[o], preferred_element_type=jnp.float32)
+        for o in range(placed_ref.shape[0])
+    )
 
 
 def sketch_terms(placed, pieces):
@@ -62,12 +62,12 @@
     return pl.pallas_call(
         sketch_kernel,
         out_shape=jax.ShapeDtypeStruct((rows, width), jnp.float32),
-        grid=(owners,),
+        grid=(rows // SKETCH_ROWS,),
         in_specs=[
-            pl.BlockSpec((1, rows, depth), lambda o: (o, 0, 0)),
-            pl.BlockSpec((1, depth, width), lambda o: (o, 0, 0)),
+            pl.BlockSpec((owners, SKETCH_ROWS, depth), lambda r: (0, r, 0)),
+            pl.BlockSpec(memory_space=pltpu.VMEM),
         ],
-        out_specs=pl.BlockSpec((rows, width), lambda o: (0, 0)),
+        out_specs=pl.BlockSpec((SKETCH_ROWS, width), lambda r: (r, 0)),
         compiler_params=pltpu.CompilerParams(vmem_limit_bytes=VMEM_BYTES),
         name="sketch_terms",
     )(placed, pieces)

time: 308 us -> 304 us (0.987)
    pallas_call x1, Pallas kernels: 21.8 us -> 18.1 us  [sketch_terms(): pl.pallas_call(sketch_kernel, out_shape=jax.ShapeDtypeStruct((rows, width...]
where the time goes in v4:
time: 304 us; the launch traced here: 302 us
  Pallas kernels  201 us (66%)
  waiting for transfers between devices  72.6 us (24%)
  local copies, waits for them, and re-layouts  11.8 us (4%)
  starting transfers between devices  6.92 us (2%)
  matrix products  6.44 us (2%)
    pallas_call x1, Pallas kernels, project_terms(): pl.pallas_call(project_kernel, out_shape=jax.ShapeDtypeStruct(shape, jnp....  98.5 us
    all_to_all x1, waiting for transfers between devices, on_device(): lax.all_to_all(local_pieces[requests], 'docs', split_axis=0, concat_axis=...  68.7 us
    pallas_call x1, Pallas kernels, inverse_factor(): pl.pallas_call(inverse_factor_kernel, out_shape=jax.ShapeDtypeStruct(gram...  27.6 us
    pallas_call x1, Pallas kernels, place_blocks(): pl.pallas_call(place_kernel, out_shape=jax.ShapeDtypeStruct(shape, blocks...  23.4 us
    pallas_call x1, Pallas kernels, sketch_terms(): pl.pallas_call(sketch_kernel, out_shape=jax.ShapeDtypeStruct((rows, width...  18.1 us
    pallas_call x1, Pallas kernels, gram_sum(): pl.pallas_call(gram_sum_kernel, out_shape=jax.ShapeDtypeStruct(parts.shap...  17.2 us
    pallas_call x1, Pallas kernels, exchange(): pl.pallas_call(exchange_kernel, out_shape=jax.ShapeDtypeStruct(value.shap...  9 us
    all_to_all x1, starting transfers between devices, on_device(): lax.all_to_all(local_pieces[requests], 'docs', split_axis=0, concat_axis=...  6.92 us
  transfers between devices with their start and end apart: 2, of which 2 were waited for; matrix products, arithmetic and copies ran while one was open for 0% of the time, Pallas kernels for 8%

profile of v4, /device:TPU:14, one launch (start us, length us, event | category | flops | bytes accessed | tf_op | source)
XLA Modules:
  0.0 301.5 jit_solution(12473084503311704730)
XLA Ops:
  0.6 0.8 copy.12
  1.4 0.6 pad.4.x_ref
  2.0 9.0 %requests.1 = s32[16,1,128]{2,1,0:T(1,128)} custom-call(s32[16,1,128]{2,1,0:T(1,128)} %pad.4.x_ref), custom_call_target="tpu_custom_call" | custom-call | tf_op jit(solution)/shard_map/requests/pallas_call | solution.py:152
  11.0 0.7 slice_reduce_fusion
  11.7 0.1 copy.13
  11.8 0.1 copy.14
  11.9 0.1 reshape.54
  12.0 5.0 %gather_fusion = bf16[64,128,256]{2,1,0:T(8,128)(2,1)} fusion(bf16[64,128,256]{2,1,0:T(8,128)(2,1)} %bitcast.16, s32[1024]{0:T(1024)S(1)} %pad_clamp_fusion), kind=kCustom, calls=%fused_computation | custom fusion | bytes 8388864 | tf_op jit(solution)/shard_map/gather | solution.py:385
  17.0 6.9 %all-to-all-start = ((bf16[16,4,128,256]{3,2,1,0:T(8,128)(2,1)}), bf16[16,4,128,256]{3,2,1,0:T(8,128)(2,1)}, u32[]{:S(2)}, u32[]{:S(2)}) async-start(bf16[16,4,128,256]{3,2,1,0:T(8,128)(2,1)} %bitcast.14), calls=%async_computation | async-start | bytes 8388608 | tf_op jit(solution)/shard_map/all_to_all | solution.py:384
  24.0 23.4 %place_blocks.1.placed_ref = bf16[16,2048,512]{2,1,0:T(8,128)(2,1)} custom-call(s32[16]{0:T(128)} %bitcast.18, s32[16,32]{1,0:T(8,128)} %entry_ref.1, bf16[16,32,128,128]{3,2,1,0:T(8,128)(2,1)} %blocks_ref.1), custom_call_target="tpu_custom_call" | custom-call | bytes 50331648 | tf_op jit(solution)/shard_map/place_blocks/pallas_call | solution.py:35
  47.4 68.7 %all-to-all-done = bf16[16,4,128,256]{3,2,1,0:T(8,128)(2,1)} async-done(((bf16[16,4,128,256]{3,2,1,0:T(8,128)(2,1)}), bf16[16,4,128,256]{3,2,1,0:T(8,128)(2,1)}, u32[]{:S(2)}, u32[]{:S(2)}) %all-to-all-start) | async-done | bytes 4194336 | tf_op jit(solution)/shard_map/all_to_all | solution.py:384
  116.1 18.1 %sketch_terms.1 = f32[2048,256]{1,0:T(8,128)} custom-call(bf16[16,2048,512]{2,1,0:T(8,128)(2,1)} %place_blocks.1.placed_ref, bf16[16,512,256]{2,1,0:T(8,128)(2,1)} %bitcast.5.pieces_ref), custom_call_target="tpu_custom_call" | custom-call | tf_op jit(solution)/shard_map/sketch_terms/pallas_call | solution.py:62
  134.1 0.6 reshape_squeeze.3.goal_ref
  134.7 3.9 %collective-permute-done = f32[2048,256]{1,0:T(8,128)} collective-permute-done((f32[2048,256]{1,0:T(8,128)}, f32[2048,256]{1,0:T(8,128)}, u32[]{:S(2)}, u32[]{:S(2)}) %collective-permute-start) | collective-permute-done | bytes 2097184 | tf_op jit(solution)/shard_map/ppermute | solution.py:391
  138.6 2.5 add.20
  141.1 3.5 %fusion = f32[256,256]{1,0:T(8,128)S(1)} fusion(f32[2048,256]{1,0:T(8,128)S(1)} %add.20), kind=kOutput, calls=%fused_computation.5 | convolution fusion | flops 1610612736 | bytes 2359296 | tf_op jit(solution)/shard_map/dot_general | solution.py:11
  144.6 0.7 reshape.50.x_ref
  145.3 17.2 %gram_sum.1 = f32[32,16,128]{2,1,0:T(8,128)} custom-call(f32[32,16,128]{2,1,0:T(8,128)} %reshape.50.x_ref), custom_call_target="tpu_custom_call" | custom-call | tf_op jit(solution)/shard_map/gram_sum/pallas_call | solution.py:306
  162.5 1.7 reshape.51.gram_ref
  164.3 27.6 %inverse_factor.1 = f32[256,256]{1,0:T(8,128)} custom-call(f32[256,256]{1,0:T(8,128)} %reshape.51.gram_ref), custom_call_target="tpu_custom_call" | custom-call | tf_op jit(solution)/shard_map/inverse_factor/pallas_call | solution.py:364
  191.9 3.0 convolution_convert_fusion
  194.9 1.4 copy.16
  196.2 98.5 %project_terms.1.incoming_ref = bf16[16,256,512]{2,1,0:T(8,128)(2,1)} custom-call(bf16[256,2048]{1,0:T(8,128)(2,1)} %bitcast.15, bf16[16,2048,512]{2,1,0:T(8,128)(2,1)} %place_blocks.1.placed_ref), custom_call_target="tpu_custom_call" | custom-call | tf_op jit(solution)/shard_map/project_terms/pallas_call | solution.py:229
  294.8 6.8 %owner_sum.1 = bf16[256,8192]{1,0:T(8,128)(2,1)} custom-call(s32[64]{0:T(128)} %reshape_squeeze.3.goal_ref, bf16[16,256,512]{2,1,0:T(8,128)(2,1)} %project_terms.1.incoming_ref), custom_call_target="tpu_custom_call" | custom-call | tf_op jit(solution)/shard_map/owner_sum/pallas_call | solution.py:96
  (5 shorter events, 0.0 us)
Async XLA Ops:
  17.0 99.0 %all-to-all-start = ((bf16[16,4,128,256]{3,2,1,0:T(8,128)(2,1)}), bf16[16,4,128,256]{3,2,1,0:T(8,128)(2,1)}, u32[]{:S(2)}, u32[]{:S(2)}) async-start(bf16[16,4,128,256]{3,2,1,0:T(8,128)(2,1)} %bitcast.14), calls=%async_computation | async-start | bytes 8388608 | tf_op jit(solution)/shard_map/all_to_all | solution.py:384
  134.1 4.5 %collective-permute-start = (f32[2048,256]{1,0:T(8,128)}, f32[2048,256]{1,0:T(8,128)}, u32[]{:S(2)}, u32[]{:S(2)}) collective-permute-start(f32[2048,256]{1,0:T(8,128)} %sketch_terms.1), channel_id=1, source_target_pairs={{0,1},{1,0},{2,3},{3,2},{4,5},{5,4},{6,7},{7,6},{8,9},{9,8},{10,11... | collective-permute-start | bytes 6291464 | tf_op jit(solution)/shard_map/ppermute | solution.py:391
  194.9 1.4 copy-start
